TPU v7x, 256 devices: a whole 4x4x8 slice. The times are simulated.
256 devices in a mesh: sub: 32 (over y, x, core), grp: 8 (over z).
Axes of the slice: x: 4, y: 4, z: 8, core: 2. Of those that a mesh axis runs over, the one named last changes fastest.
Arguments:
- residual: bfloat16 [8, 32, 1024, 512], P('grp', 'sub'), may hold values from -6 to 6
- face_order: int32 [8, 32, 1024], P('grp', 'sub'), may hold values from 0 to 1023, each once within a row
- stiffness: float32 [8, 32], replicated, may hold values from 1 to 100
- schur: bfloat16 [8, 32, 1024, 1024], P('grp', 'sub')
- local_inverse: bfloat16 [8, 32, 1024, 1024], P('grp', 'sub')
- coarse_basis: bfloat16 [8, 32, 1024, 128], P('grp', 'sub'), may hold values from -0.1875 to 0.1875
- coarse_map: int32 [8, 32, 128], P('grp', 'sub'), may hold values from 0 to 511, as said below
- level2_inverse: float32 [8, 512, 512], P('grp')
- level2_basis: float32 [8, 512, 128], P('grp'), may hold values from -0.25 to 0.25
- level2_map: int32 [8, 128], P('grp'), may hold values from 0 to 511, as said below
- level3_inverse: float32 [512, 512], replicated
Outputs:
- solution: bfloat16 [8, 32, 1024, 512], P('grp', 'sub')
- image: bfloat16 [8, 32, 1024, 512], P('grp', 'sub')
Inputs may be any that keep to these rules, and one draw needn't show every extreme that they name: `face_order`: each subdomain's row holds every number of 0 to 1023 once. `coarse_map`: within one subdomain the 128 entries are distinct, and each of a group's 512 level-2 coarse values is named by some subdomain of the group. `level2_map`: within one group the 128 entries are distinct, and each level-3 coarse value is named by some group.
All inputs are finite; a program needn't handle non-finite values.
Results may differ from a plain program's by a relative error of at most 0.0062.
Values may be sent and summed in bfloat16 or wider, within the bound.
A program may use at most 64 MiB of HBM per device.

v0:
```python
import jax
import jax.numpy as jnp
from jax import lax
from jax.sharding import PartitionSpec as P

highest = lax.Precision.HIGHEST


def extended(cells, sides, width):
    for axis, dim in sides:
        count = lax.axis_size(axis)
        ends = count - 1
        head = lax.slice_in_dim(cells, 0, width, axis=dim)
        tail = lax.slice_in_dim(cells, cells.shape[dim] - width, cells.shape[dim], axis=dim)
        cells = jnp.concatenate(
            [
                lax.ppermute(tail, axis, [(i, (i + 1) % count) for i in range(ends)]),
                cells,
                lax.ppermute(head, axis, [((i + 1) % count, i) for i in range(ends)]),
            ],
            axis=dim,
        )
    return cells


def face_weights(stiffness, group_index, member_index):
    group_count, member_count = stiffness.shape
    itself = stiffness[group_index, member_index]

    def share_of(other_group, other_member, present):
        neighbour = stiffness[
            jnp.clip(other_group, 0, group_count - 1), jnp.clip(other_member, 0, member_count - 1)
        ]
        return jnp.where(present, itself / (itself + neighbour), jnp.float32(1.0))

    return jnp.stack(
        [
            share_of(group_index, member_index - 1, member_index > 0),
            share_of(group_index, member_index + 1, member_index < member_count - 1),
            share_of(group_index - 1, member_index, group_index > 0),
            share_of(group_index + 1, member_index, group_index < group_count - 1),
        ]
    )


def shards(
    residual,
    face_order,
    stiffness,
    schur,
    local_inverse,
    coarse_basis,
    coarse_map,
    level2_inverse,
    level2_basis,
    level2_map,
    level3_inverse,
):
    resid_block = residual[0, 0]
    interface_size, columns = resid_block.shape
    face_size = interface_size // 4
    ordering = face_order[0, 0]
    inverse = jnp.argsort(ordering)
    group_index = lax.axis_index("grp")
    member_index = lax.axis_index("sub")
    weights = face_weights(stiffness, group_index, member_index)
    face_of = inverse // face_size
    dof_weight = jnp.sum(
        jnp.where(face_of[:, None] == jnp.arange(4)[None, :], weights[None, :], jnp.float32(0.0)),
        axis=1,
    )
    weighted = (dof_weight[:, None] * resid_block.astype(jnp.float32)).astype(jnp.bfloat16)
    contract_rows = (((0,), (0,)), ((), ()))
    coarse_base = coarse_basis[0, 0]
    coarse_res = lax.dot_general(
        coarse_base, weighted, contract_rows, preferred_element_type=jnp.float32
    )
    level2_size = level2_inverse.shape[1]
    local_map = coarse_map[0, 0]
    selector = (local_map[None, :] == jnp.arange(level2_size)[:, None]).astype(jnp.float32)
    contribution = jnp.dot(selector, coarse_res, precision=highest)
    group_base = level2_basis[0]
    group_map = level2_map[0]
    level3_size = level3_inverse.shape[0]
    selector_three = (group_map[None, :] == jnp.arange(level3_size)[:, None]).astype(jnp.float32)
    local_part = jnp.dot(local_inverse[0, 0], weighted, preferred_element_type=jnp.float32)
    group_inverse = level2_inverse[0]
    level2_res = lax.psum(contribution, "sub")
    group_terms = lax.dot_general(group_base, level2_res, contract_rows, precision=highest)
    level3_res = lax.psum(jnp.dot(selector_three, group_terms, precision=highest), "grp")
    level2_local = jnp.dot(group_inverse, level2_res, precision=highest)
    level3_sol = jnp.dot(level3_inverse, level3_res, precision=highest)
    level2_sol = level2_local + jnp.dot(group_base, level3_sol[group_map], precision=highest)
    coarse_part = jnp.dot(coarse_base.astype(jnp.float32), level2_sol[local_map], precision=highest)
    sendable = (dof_weight[:, None] * (local_part + coarse_part)).astype(jnp.bfloat16)
    face_blocks = sendable[ordering].reshape(4, face_size, columns)
    sub_padded = extended(face_blocks[0:2], (("sub", 0),), 1)
    grp_padded = extended(face_blocks[2:4], (("grp", 0),), 1)
    received = jnp.stack([sub_padded[0], sub_padded[3], grp_padded[0], grp_padded[3]])
    summed = (face_blocks.astype(jnp.float32) + received.astype(jnp.float32)).astype(jnp.bfloat16)
    solution = summed.reshape(interface_size, columns)[inverse]
    image = jnp.dot(schur[0, 0], solution, preferred_element_type=jnp.float32).astype(jnp.bfloat16)
    return (solution[None, None], image[None, None])


def solution(mesh):
    placed = (
        P("grp", "sub", None, None),
        P("grp", "sub", None),
        P(),
        P("grp", "sub", None, None),
        P("grp", "sub", None, None),
        P("grp", "sub", None, None),
        P("grp", "sub", None),
        P("grp", None, None),
        P("grp", None, None),
        P("grp", None),
        P(),
    )
    return jax.shard_map(
        shards,
        mesh=mesh,
        in_specs=placed,
        out_specs=(P("grp", "sub", None, None), P("grp", "sub", None, None)),
        check_vma=False,
    )
```

profile of v0, /device:TPU:8, one launch (start us, length us, event | category | flops | bytes accessed | tf_op | source)
XLA Modules:
  0.0 290.3 jit_solution(15084661443975097650)
XLA Ops:
  7.2 0.0 copy-start
  7.2 0.0 all-reduce.3.cloned.1.call-start
  7.2 1.6 fusion.33
  16.3 5.1 %sort.17 = (s32[1024]{0:T(1024)}, s32[1024]{0:T(1024)S(1)}) sort(s32[1024]{0:T(1024)} %bitcast.82, s32[1024]{0:T(1024)S(1)} %iota.13), dimensions={0}, to_apply=%region_0.0 | sort | flops 10240 | bytes 16384 | tf_op jit(solution)/shard_map/jit(argsort)/sort | solution.py:63
  21.4 0.0 copy-start.6
  21.4 0.1 pad_maximum_fusion.1
  21.5 0.1 select_reduce_fusion
  21.6 1.9 fusion.15
  23.6 2.2 fusion.24
  25.8 0.0 all-reduce.3.cloned.1.call-update
  25.8 0.0 copy-start.7
  25.8 0.0 copy-start.5
  25.8 0.0 all-reduce.5.cloned.1.call-start
  25.9 0.0 copy-done.6
  25.9 117.2 %all-reduce.3.cloned.1.call-done = f32[512,512]{1,0:T(8,128)} async-done(((f32[512,512]{1,0:T(8,128)}), f32[512,512]{1,0:T(8,128)}) %all-reduce.3.cloned.1.call-update) | async-done | bytes 1048592 | tf_op jit(solution)/shard_map/psum | solution.py:88
  143.2 0.0 copy-done.4
  143.2 3.0 %fusion.20 = f32[512,128]{1,0:T(8,128)S(1)} fusion(f32[512,512]{1,0:T(8,128)} %all-reduce.3.cloned.1.call-done, f32[1,512,128]{2,1,0:T(8,128)S(1)} %copy-done.4), kind=kOutput, calls=%fused_computation.28 | convolution fusion | flops 402653184 | bytes 1572864 | tf_op jit(solution)/shard_map/dot_general | solution.py:89
  146.2 1.6 fusion.25
  147.8 0.0 all-reduce.5.cloned.1.call-update
  147.8 0.0 copy-done.7
  147.8 0.0 copy-done.5
  147.9 0.0 copy-start.3
  147.9 4.2 %fusion.3 = f32[512,1024]{1,0:T(8,128)} fusion(bf16[1,1,1024,1024]{3,2,1,0:T(8,128)(2,1)S(1)} %copy-done, bf16[1,1,1024,512]{3,2,1,0:T(8,128)(2,1)} %param.11, f32[1024]{0:T(1024)S(1)} %select_reduce_fusion), kind=kOutput, calls=%fused_computation.8 | convolution fusion | flops 1075314688 | bytes 5246976 | tf_op jit(solution)/shard_map/dot_general | solution.py:86
  152.1 72.2 %all-reduce.5.cloned.1.call-done = f32[512,512]{1,0:T(8,128)} async-done(((f32[512,512]{1,0:T(8,128)}), f32[512,512]{1,0:T(8,128)}) %all-reduce.5.cloned.1.call-update) | async-done | bytes 1048592 | tf_op jit(solution)/shard_map/psum | solution.py:90
  224.3 5.7 %convolution_bitcast_fusion = f32[512,512]{0,1:T(8,128)} fusion(f32[512,512]{1,0:T(8,128)} %all-reduce.5.cloned.1.call-done, f32[512,512]{1,0:T(8,128)S(1)} %copy-done.3), kind=kOutput, calls=%fused_computation.15 | convolution fusion | flops 1610612736 | bytes 3145728 | tf_op jit(solution)/shard_map/dot_general | solution.py:92
  230.0 1.6 copy.17
  231.5 0.8 gather_fusion
  232.3 2.1 fusion.18
  234.4 5.7 %fusion.12 = f32[512,512]{0,1:T(8,128)} fusion(f32[512,512]{1,0:T(8,128)S(1)} %fusion.18, f32[512,512]{1,0:T(8,128)S(1)} %copy-done.2, f32[1,512,512]{2,1,0:T(8,128)} %param.18), kind=kOutput, calls=%fused_computation.17 | convolution fusion | flops 1610874880 | bytes 4194304 | tf_op jit(solution)/shard_map/dot_general | solution.py:91
  240.1 1.7 copy.18
  241.8 0.8 gather_fusion.1
  242.5 3.7 %fusion.11 = bf16[1024,512]{0,1:T(8,128)(2,1)} fusion(f32[512,1024]{1,0:T(8,128)} %fusion.3, f32[128,512]{1,0:T(8,128)S(1)} %gather_fusion.1, f32[1024]{0:T(1024)S(1)} %select_reduce_fusion, bf16[1,1,1024,128]{3,2,1,0:T(8,128)(2,1)} %param.16), kind=kOutput, calls=%fused_computation.14 | convolution fusion | flops 806879232 | bytes 3674112 | tf_op jit(solution)/shard_map/dot_general | solution.py:94
  246.3 1.5 copy.19
  247.8 5.1 %gather_fusion.2 = bf16[1024,512]{1,0:T(8,128)(2,1)} fusion(bf16[1024,512]{1,0:T(8,128)(2,1)S(1)} %copy.19, s32[1024]{0:T(1024)S(1)} %broadcast_clamp_fusion), kind=kCustom, calls=%fused_computation.2 | custom fusion | bytes 2101248 | tf_op jit(solution)/shard_map/gather | solution.py:96
  252.9 1.3 slice_bitcast_fusion.3
  254.2 1.9 collective-permute-start
  256.2 5.8 %collective-permute-start.1 = (bf16[1,256,512]{2,1,0:T(8,128)(2,1)S(1)}, bf16[1,256,512]{2,1,0:T(8,128)(2,1)S(1)}, u32[]{:S(2)}, u32[]{:S(2)}) collective-permute-start(bf16[1,256,512]{2,1,0:T(8,128)(2,1)S(1)} %get-tuple-element.12), channel_id=1, source_target_pairs={{8,0},{16,8},{24,16},{32,24},{40,32},{48,40},{56,48},{64,56},{72,6... | collective-permute-start | bytes 786440 | tf_op jit(solution)/shard_map/ppermute | solution.py:19
  261.9 3.1 %collective-permute-start.2 = (bf16[1,256,512]{2,1,0:T(8,128)(2,1)S(1)}, bf16[1,256,512]{2,1,0:T(8,128)(2,1)S(1)}, u32[]{:S(2)}, u32[]{:S(2)}) collective-permute-start(bf16[1,256,512]{2,1,0:T(8,128)(2,1)S(1)} %get-tuple-element.11), channel_id=1, source_target_pairs={{0,1},{1,2},{2,3},{3,4},{4,5},{5,6},{6,7},{8,9},{9,10},{10,11},{11... | collective-permute-start | bytes 786440 | tf_op jit(solution)/shard_map/ppermute | solution.py:17
  265.1 1.3 collective-permute-start.3
  266.4 0.0 collective-permute-done
  266.4 0.0 collective-permute-done.1
  266.4 2.5 collective-permute-done.2
  268.9 4.4 %collective-permute-done.3 = bf16[1,256,512]{2,1,0:T(8,128)(2,1)S(1)} collective-permute-done((bf16[1,256,512]{2,1,0:T(8,128)(2,1)S(1)}, bf16[1,256,512]{2,1,0:T(8,128)(2,1)S(1)}, u32[]{:S(2)}, u32[]{:S(2)}) %collective-permute-start.3) | collective-permute-done | bytes 262176 | tf_op jit(solution)/shard_map/ppermute | solution.py:19
  273.3 0.1 pad_maximum_fusion
  273.5 0.4 fusion
  273.9 5.1 %gather_fusion.3 = bf16[1024,512]{1,0:T(8,128)(2,1)} fusion(bf16[1024,512]{1,0:T(8,128)(2,1)S(1)} %fusion, s32[1024]{0:T(1024)S(1)} %get-tuple-element.14), kind=kCustom, calls=%fused_computation.3 | custom fusion | bytes 2101248 | tf_op jit(solution)/shard_map/gather | solution.py:101
  278.9 3.2 %fusion.8 = bf16[1,1,1024,512]{2,3,1,0:T(8,128)(2,1)S(1)} fusion(bf16[1024,512]{1,0:T(8,128)(2,1)} %gather_fusion.3, bf16[1,1,1024,1024]{3,2,1,0:T(8,128)(2,1)} %param.14), kind=kOutput, calls=%fused_computation.13 | convolution fusion | flops 1074266112 | bytes 4194304 | tf_op jit(solution)/shard_map/dot_general | solution.py:102
  282.2 1.3 copy.20
  (15 shorter events, 0.1 us)
Async XLA Ops:
  7.2 140.7 %copy-start = (bf16[1,1,1024,1024]{3,2,1,0:T(8,128)(2,1)S(1)}, bf16[1,1,1024,1024]{3,2,1,0:T(8,128)(2,1)}, u32[]{:S(2)}) copy-start(bf16[1,1,1024,1024]{3,2,1,0:T(8,128)(2,1)} %param.15) | copy-start | bytes 6291460
  7.2 136.0 %all-reduce.3.cloned.1.call-start = ((), (), s32[]{:S(2)}) async-start(), calls=%async_computation | async-start | bytes 2097152 | tf_op jit(solution)/shard_map/psum | solution.py:88
  21.4 4.5 %copy-start.6 = (s32[1,128]{1,0:T(1,128)S(1)}, s32[1,128]{1,0:T(1,128)}, u32[]{:S(2)}) copy-start(s32[1,128]{1,0:T(1,128)} %param.20) | copy-start | bytes 1540
  21.5 121.6 %copy-start.4 = (f32[1,512,128]{2,1,0:T(8,128)S(1)}, f32[1,512,128]{2,1,0:T(8,128)}, u32[]{:S(2)}) copy-start(f32[1,512,128]{2,1,0:T(8,128)} %param.19) | copy-start | bytes 786436
  25.8 122.0 %copy-start.7 = (s32[1,1,128]{2,1,0:T(1,128)S(1)}, s32[1,1,128]{2,1,0:T(1,128)}, u32[]{:S(2)}) copy-start(s32[1,1,128]{2,1,0:T(1,128)} %param.17) | copy-start | bytes 1540
  25.8 122.0 %copy-start.5 = (s32[1,1,1024]{2,1,0:T(1,128)S(1)}, s32[1,1,1024]{2,1,0:T(1,128)}, u32[]{:S(2)}) copy-start(s32[1,1,1024]{2,1,0:T(1,128)} %param.12) | copy-start | bytes 12292
  25.8 198.5 %all-reduce.5.cloned.1.call-start = ((), (), s32[]{:S(2)}) async-start(), calls=%async_computation.1 | async-start | bytes 2097152 | tf_op jit(solution)/shard_map/psum | solution.py:90
  147.9 76.4 %copy-start.3 = (f32[512,512]{1,0:T(8,128)S(1)}, f32[512,512]{1,0:T(8,128)}, u32[]{:S(2)}) copy-start(f32[512,512]{1,0:T(8,128)} %param.21) | copy-start | bytes 3145732
  232.3 2.1 copy-start.2
  252.9 20.6 %copy-start.1 = (bf16[1024,512]{1,0:T(8,128)(2,1)S(1)}, bf16[1024,512]{1,0:T(8,128)(2,1)}, u32[]{:S(2)}) copy-start(bf16[1024,512]{1,0:T(8,128)(2,1)} %gather_fusion.2) | copy-start | bytes 3145732
  254.2 12.1 %collective-permute-start = (bf16[1,256,512]{2,1,0:T(8,128)(2,1)S(1)}, bf16[1,256,512]{2,1,0:T(8,128)(2,1)S(1)}, u32[]{:S(2)}, u32[]{:S(2)}) collective-permute-start(bf16[1,256,512]{2,1,0:T(8,128)(2,1)S(1)} %get-tuple-element.10), channel_id=1, source_target_pairs={{0,8},{8,16},{16,24},{24,32},{32,40},{40,48},{48,56},{56,64},{64,7... | collective-permute-start | bytes 786440 | tf_op jit(solution)/shard_map/ppermute | solution.py:17
  256.2 10.2 %collective-permute-start.1 = (bf16[1,256,512]{2,1,0:T(8,128)(2,1)S(1)}, bf16[1,256,512]{2,1,0:T(8,128)(2,1)S(1)}, u32[]{:S(2)}, u32[]{:S(2)}) collective-permute-start(bf16[1,256,512]{2,1,0:T(8,128)(2,1)S(1)} %get-tuple-element.12), channel_id=1, source_target_pairs={{8,0},{16,8},{24,16},{32,24},{40,32},{48,40},{56,48},{64,56},{72,6... | collective-permute-start | bytes 786440 | tf_op jit(solution)/shard_map/ppermute | solution.py:19
  261.9 7.0 %collective-permute-start.2 = (bf16[1,256,512]{2,1,0:T(8,128)(2,1)S(1)}, bf16[1,256,512]{2,1,0:T(8,128)(2,1)S(1)}, u32[]{:S(2)}, u32[]{:S(2)}) collective-permute-start(bf16[1,256,512]{2,1,0:T(8,128)(2,1)S(1)} %get-tuple-element.11), channel_id=1, source_target_pairs={{0,1},{1,2},{2,3},{3,4},{4,5},{5,6},{6,7},{8,9},{9,10},{10,11},{11... | collective-permute-start | bytes 786440 | tf_op jit(solution)/shard_map/ppermute | solution.py:17
  265.1 8.3 %collective-permute-start.3 = (bf16[1,256,512]{2,1,0:T(8,128)(2,1)S(1)}, bf16[1,256,512]{2,1,0:T(8,128)(2,1)S(1)}, u32[]{:S(2)}, u32[]{:S(2)}) collective-permute-start(bf16[1,256,512]{2,1,0:T(8,128)(2,1)S(1)} %get-tuple-element.13), channel_id=1, source_target_pairs={{1,0},{2,1},{3,2},{4,3},{5,4},{6,5},{7,6},{9,8},{10,9},{11,10},{12... | collective-permute-start | bytes 786440 | tf_op jit(solution)/shard_map/ppermute | solution.py:19
Sparse Core Ops, SparseCore 0:
  25.9 117.1 all-reduce.2
  147.9 76.3 all-reduce.4
where the time goes:
time: 291 us; the launch traced here: 290 us
  waiting for transfers between devices  196 us (67%)
  matrix products  33.3 us (11%)
  between operations  21.9 us (8%)
  local copies, waits for them, and re-layouts  20.7 us (7%)
  starting transfers between devices  12.2 us (4%)
  other arithmetic  5.76 us (2%)
    psum x1, waiting for transfers between devices, shards(): level2_res = lax.psum(contribution, 'sub')  117 us
    psum x1, waiting for transfers between devices, shards(): lax.psum(jnp.dot(selector_three, group_terms, precision=highest), 'grp')  72.2 us
    ppermute x2, starting transfers between devices, extended(): lax.ppermute(head, axis, [((i + 1) % count, i) for i in range(ends)])  7.04 us
  transfers between devices with their start and end apart: 6, of which 4 were waited for; matrix products, arithmetic and copies ran while one was open for 1% of the time, Pallas kernels for 0%

commit v1 on v0

--- a/solution.py
+++ b/solution.py
@@ -85,7 +85,13 @@
     selector_three = (group_map[None, :] == jnp.arange(level3_size)[:, None]).astype(jnp.float32)
     local_part = jnp.dot(local_inverse[0, 0], weighted, preferred_element_type=jnp.float32)
     group_inverse = level2_inverse[0]
-    level2_res = lax.psum(contribution, "sub")
+    many = lax.axis_size("sub")
+    level2_res = contribution
+    for num in [
+        [(jj, jj ^ tick) for jj in range(many)] for tick in (1, 2, 4, 8, 16) if tick < many
+    ]:
+        mixed_arr = lax.ppermute(level2_res, axis_name="sub", perm=num)
+        level2_res = level2_res + mixed_arr
     group_terms = lax.dot_general(group_base, level2_res, contract_rows, precision=highest)
     level3_res = lax.psum(jnp.dot(selector_three, group_terms, precision=highest), "grp")
     level2_local = jnp.dot(group_inverse, level2_res, precision=highest)

time: 291 us -> 281 us (0.966)
  waiting for transfers between devices: 196 us -> 174 us
  starting transfers between devices: 12.2 us -> 21.3 us
  local copies, waits for them, and re-layouts: 20.7 us -> 24.5 us
    psum x1 -> x0, waiting for transfers between devices: 117 us -> none  [shards(): level2_res = lax.psum(contribution, 'sub')]
    ppermute x0 -> x5, waiting for transfers between devices: none -> 93.4 us  [shards(): mixed_arr = lax.ppermute(level2_res, axis_name='sub', perm=num)]
    ppermute x0 -> x5, starting transfers between devices: none -> 9.16 us  [shards(): mixed_arr = lax.ppermute(level2_res, axis_name='sub', perm=num)]
  transfers between devices with their start and end apart: 6 -> 10, of which waited for: 4 -> 8; matrix products, arithmetic and copies ran while one was open for 1% -> 1% of each run, Pallas kernels for 0% -> 0%
where the time goes in v1:
time: 281 us; the launch traced here: 280 us
  waiting for transfers between devices  174 us (62%)
  matrix products  31.6 us (11%)
  local copies, waits for them, and re-layouts  24.5 us (9%)
  between operations  21.9 us (8%)
  starting transfers between devices  21.3 us (8%)
  other arithmetic  6.59 us (2%)
    ppermute x5, waiting for transfers between devices, shards(): mixed_arr = lax.ppermute(level2_res, axis_name='sub', perm=num)  93.4 us
    psum x1, waiting for transfers between devices, shards(): lax.psum(jnp.dot(selector_three, group_terms, precision=highest), 'grp')  74 us
    ppermute x5, starting transfers between devices, shards(): mixed_arr = lax.ppermute(level2_res, axis_name='sub', perm=num)  9.16 us
    ppermute x2, starting transfers between devices, extended(): lax.ppermute(head, axis, [((i + 1) % count, i) for i in range(ends)])  7.04 us
    dot_general x1, matrix products, shards(): level3_sol = jnp.dot(level3_inverse, level3_res, precision=highest)  5.98 us
    dot_general x1, matrix products, shards(): level2_local = jnp.dot(group_inverse, level2_res, precision=highest)  5.9 us
  transfers between devices with their start and end apart: 10, of which 8 were waited for; matrix products, arithmetic and copies ran while one was open for 1% of the time, Pallas kernels for 0%

profile of v1, /device:TPU:8, one launch (start us, length us, event | category | flops | bytes accessed | tf_op | source)
XLA Modules:
  0.0 280.2 jit_solution(16596304576287825161)
XLA Ops:
  7.2 0.0 all-reduce.2.cloned.1.call-start
  7.2 1.6 fusion.35
  16.4 5.1 %sort.17 = (s32[1024]{0:T(1024)}, s32[1024]{0:T(1024)S(1)}) sort(s32[1024]{0:T(1024)} %bitcast.80, s32[1024]{0:T(1024)S(1)} %iota.13), dimensions={0}, to_apply=%region_0.0 | sort | flops 10240 | bytes 16384 | tf_op jit(solution)/shard_map/jit(argsort)/sort | solution.py:63
  21.5 0.1 pad_maximum_fusion.1
  21.6 0.1 select_reduce_fusion
  21.6 1.9 fusion.18
  23.6 1.3 fusion.26
  24.9 0.1 collective-permute-start
  25.0 2.6 collective-permute-done
  27.6 0.2 add.107
  27.8 1.6 collective-permute-start.1
  29.4 23.7 %collective-permute-done.1 = f32[512,512]{1,0:T(8,128)S(1)} collective-permute-done((f32[512,512]{1,0:T(8,128)S(1)}, f32[512,512]{1,0:T(8,128)S(1)}, u32[]{:S(2)}, u32[]{:S(2)}) %collective-permute-start.1) | collective-permute-done | bytes 1048608 | tf_op jit(solution)/shard_map/ppermute | solution.py:93
  53.1 0.2 add.108
  53.3 3.1 %collective-permute-start.2 = (f32[512,512]{1,0:T(8,128)S(1)}, f32[512,512]{1,0:T(8,128)S(1)}, u32[]{:S(2)}, u32[]{:S(2)}) collective-permute-start(f32[512,512]{1,0:T(8,128)S(1)} %add.108), channel_id=1, source_target_pairs={{0,32},{8,40},{16,48},{24,56},{32,0},{40,8},{48,16},{56,24},{64,96... | collective-permute-start | bytes 3145736 | tf_op jit(solution)/shard_map/ppermute | solution.py:93
  56.4 22.9 %collective-permute-done.2 = f32[512,512]{1,0:T(8,128)S(1)} collective-permute-done((f32[512,512]{1,0:T(8,128)S(1)}, f32[512,512]{1,0:T(8,128)S(1)}, u32[]{:S(2)}, u32[]{:S(2)}) %collective-permute-start.2) | collective-permute-done | bytes 1048608 | tf_op jit(solution)/shard_map/ppermute | solution.py:93
  79.3 0.2 add.109
  79.5 2.3 collective-permute-start.3
  81.8 21.7 %collective-permute-done.3 = f32[512,512]{1,0:T(8,128)S(1)} collective-permute-done((f32[512,512]{1,0:T(8,128)S(1)}, f32[512,512]{1,0:T(8,128)S(1)}, u32[]{:S(2)}, u32[]{:S(2)}) %collective-permute-start.3) | collective-permute-done | bytes 1048608 | tf_op jit(solution)/shard_map/ppermute | solution.py:93
  103.5 0.2 add.110
  103.7 2.1 collective-permute-start.4
  105.8 22.4 %collective-permute-done.4 = f32[512,512]{1,0:T(8,128)S(1)} collective-permute-done((f32[512,512]{1,0:T(8,128)S(1)}, f32[512,512]{1,0:T(8,128)S(1)}, u32[]{:S(2)}, u32[]{:S(2)}) %collective-permute-start.4) | collective-permute-done | bytes 1048608 | tf_op jit(solution)/shard_map/ppermute | solution.py:93
  128.3 1.0 copy-done.2
  129.3 1.8 fusion.15
  131.1 1.6 fusion.27
  132.8 4.1 %fusion.3 = f32[512,1024]{1,0:T(8,128)} fusion(bf16[1,1,1024,1024]{3,2,1,0:T(8,128)(2,1)S(1)} %copy-done, bf16[1,1,1024,512]{3,2,1,0:T(8,128)(2,1)} %param.11, f32[1024]{0:T(1024)S(1)} %select_reduce_fusion), kind=kOutput, calls=%fused_computation.8 | convolution fusion | flops 1075314688 | bytes 5246976 | tf_op jit(solution)/shard_map/dot_general | solution.py:86
  136.9 74.0 %all-reduce.2.cloned.1.call-done = f32[512,512]{1,0:T(8,128)} async-done(((f32[512,512]{1,0:T(8,128)}), f32[512,512]{1,0:T(8,128)}) %all-reduce.2.cloned.1.call-update) | async-done | bytes 1048592 | tf_op jit(solution)/shard_map/psum | solution.py:96
  210.8 6.0 %convolution_bitcast_fusion = f32[512,512]{0,1:T(8,128)} fusion(f32[512,512]{1,0:T(8,128)} %all-reduce.2.cloned.1.call-done, f32[512,512]{1,0:T(8,128)} %param.21), kind=kOutput, calls=%fused_computation.15 | convolution fusion | flops 1610612736 | bytes 3145728 | tf_op jit(solution)/shard_map/dot_general | solution.py:98
  216.8 2.5 copy.17
  219.4 2.8 gather_fusion
  222.1 2.1 fusion.21
  224.2 5.9 %fusion.12 = f32[512,512]{0,1:T(8,128)} fusion(f32[512,512]{1,0:T(8,128)S(1)} %fusion.21, f32[1,512,512]{2,1,0:T(8,128)} %param.18, f32[512,512]{1,0:T(8,128)S(1)} %add.110, f32[512,512]{1,0:T(8,128)S(1)} %copy-done.3), kind=kOutput, calls=%fused_computation.17 | convolution fusion | flops 1611137024 | bytes 5242880 | tf_op jit(solution)/shard_map/dot_general | solution.py:97
  230.1 1.6 copy.18
  231.7 0.8 gather_fusion.1
  232.4 3.7 %fusion.11 = bf16[1024,512]{0,1:T(8,128)(2,1)} fusion(f32[512,1024]{1,0:T(8,128)} %fusion.3, f32[128,512]{1,0:T(8,128)S(1)} %gather_fusion.1, f32[1024]{0:T(1024)S(1)} %select_reduce_fusion, bf16[1,1,1024,128]{3,2,1,0:T(8,128)(2,1)} %param.16), kind=kOutput, calls=%fused_computation.14 | convolution fusion | flops 806879232 | bytes 3674112 | tf_op jit(solution)/shard_map/dot_general | solution.py:100
  236.2 1.5 copy.19
  237.7 5.1 %gather_fusion.2 = bf16[1024,512]{1,0:T(8,128)(2,1)} fusion(bf16[1024,512]{1,0:T(8,128)(2,1)S(1)} %copy.19, s32[1024]{0:T(1024)S(1)} %broadcast_clamp_fusion), kind=kCustom, calls=%fused_computation.2 | custom fusion | bytes 2101248 | tf_op jit(solution)/shard_map/gather | solution.py:102
  242.8 1.3 slice_bitcast_fusion.3
  244.1 1.9 collective-permute-start.5
  246.1 5.8 %collective-permute-start.6 = (bf16[1,256,512]{2,1,0:T(8,128)(2,1)S(1)}, bf16[1,256,512]{2,1,0:T(8,128)(2,1)S(1)}, u32[]{:S(2)}, u32[]{:S(2)}) collective-permute-start(bf16[1,256,512]{2,1,0:T(8,128)(2,1)S(1)} %get-tuple-element.12), channel_id=1, source_target_pairs={{8,0},{16,8},{24,16},{32,24},{40,32},{48,40},{56,48},{64,56},{72,6... | collective-permute-start | bytes 786440 | tf_op jit(solution)/shard_map/ppermute | solution.py:19
  251.8 3.2 %collective-permute-start.7 = (bf16[1,256,512]{2,1,0:T(8,128)(2,1)S(1)}, bf16[1,256,512]{2,1,0:T(8,128)(2,1)S(1)}, u32[]{:S(2)}, u32[]{:S(2)}) collective-permute-start(bf16[1,256,512]{2,1,0:T(8,128)(2,1)S(1)} %get-tuple-element.11), channel_id=1, source_target_pairs={{0,1},{1,2},{2,3},{3,4},{4,5},{5,6},{6,7},{8,9},{9,10},{10,11},{11... | collective-permute-start | bytes 786440 | tf_op jit(solution)/shard_map/ppermute | solution.py:17
  255.0 1.3 collective-permute-start.8
  256.3 2.5 collective-permute-done.7
  258.8 4.4 %collective-permute-done.8 = bf16[1,256,512]{2,1,0:T(8,128)(2,1)S(1)} collective-permute-done((bf16[1,256,512]{2,1,0:T(8,128)(2,1)S(1)}, bf16[1,256,512]{2,1,0:T(8,128)(2,1)S(1)}, u32[]{:S(2)}, u32[]{:S(2)}) %collective-permute-start.8) | collective-permute-done | bytes 262176 | tf_op jit(solution)/shard_map/ppermute | solution.py:19
  263.2 0.1 pad_maximum_fusion
  263.4 0.4 fusion
  263.8 5.1 %gather_fusion.3 = bf16[1024,512]{1,0:T(8,128)(2,1)} fusion(bf16[1024,512]{1,0:T(8,128)(2,1)S(1)} %fusion, s32[1024]{0:T(1024)S(1)} %get-tuple-element.14), kind=kCustom, calls=%fused_computation.3 | custom fusion | bytes 2101248 | tf_op jit(solution)/shard_map/gather | solution.py:107
  268.8 3.2 %fusion.8 = bf16[1,1,1024,512]{2,3,1,0:T(8,128)(2,1)S(1)} fusion(bf16[1024,512]{1,0:T(8,128)(2,1)} %gather_fusion.3, bf16[1,1,1024,1024]{3,2,1,0:T(8,128)(2,1)} %param.14), kind=kOutput, calls=%fused_computation.13 | convolution fusion | flops 1074266112 | bytes 4194304 | tf_op jit(solution)/shard_map/dot_general | solution.py:108
  272.1 1.3 copy.20
  (26 shorter events, 0.1 us)
Async XLA Ops:
  7.2 125.6 %copy-start = (bf16[1,1,1024,1024]{3,2,1,0:T(8,128)(2,1)S(1)}, bf16[1,1,1024,1024]{3,2,1,0:T(8,128)(2,1)}, u32[]{:S(2)}) copy-start(bf16[1,1,1024,1024]{3,2,1,0:T(8,128)(2,1)} %param.15) | copy-start | bytes 6291460
  7.2 203.7 %all-reduce.2.cloned.1.call-start = ((), (), s32[]{:S(2)}) async-start(), calls=%async_computation | async-start | bytes 2097152 | tf_op jit(solution)/shard_map/psum | solution.py:96
  24.9 2.7 collective-permute-start
  27.8 25.3 %collective-permute-start.1 = (f32[512,512]{1,0:T(8,128)S(1)}, f32[512,512]{1,0:T(8,128)S(1)}, u32[]{:S(2)}, u32[]{:S(2)}) collective-permute-start(f32[512,512]{1,0:T(8,128)S(1)} %add.107), channel_id=1, source_target_pairs={{0,16},{8,24},{16,0},{24,8},{32,48},{40,56},{48,32},{56,40},{64,80... | collective-permute-start | bytes 3145736 | tf_op jit(solution)/shard_map/ppermute | solution.py:93
  53.3 26.0 %collective-permute-start.2 = (f32[512,512]{1,0:T(8,128)S(1)}, f32[512,512]{1,0:T(8,128)S(1)}, u32[]{:S(2)}, u32[]{:S(2)}) collective-permute-start(f32[512,512]{1,0:T(8,128)S(1)} %add.108), channel_id=1, source_target_pairs={{0,32},{8,40},{16,48},{24,56},{32,0},{40,8},{48,16},{56,24},{64,96... | collective-permute-start | bytes 3145736 | tf_op jit(solution)/shard_map/ppermute | solution.py:93
  79.5 26.3 %copy-start.6 = (s32[1,128]{1,0:T(1,128)S(1)}, s32[1,128]{1,0:T(1,128)}, u32[]{:S(2)}) copy-start(s32[1,128]{1,0:T(1,128)} %param.20) | copy-start | bytes 1540
  79.5 49.8 %copy-start.4 = (f32[1,512,128]{2,1,0:T(8,128)S(1)}, f32[1,512,128]{2,1,0:T(8,128)}, u32[]{:S(2)}) copy-start(f32[1,512,128]{2,1,0:T(8,128)} %param.19) | copy-start | bytes 786436
  79.5 24.0 %collective-permute-start.3 = (f32[512,512]{1,0:T(8,128)S(1)}, f32[512,512]{1,0:T(8,128)S(1)}, u32[]{:S(2)}, u32[]{:S(2)}) collective-permute-start(f32[512,512]{1,0:T(8,128)S(1)} %add.109), channel_id=1, source_target_pairs={{0,64},{8,72},{16,80},{24,88},{32,96},{40,104},{48,112},{56,120},{... | collective-permute-start | bytes 3145736 | tf_op jit(solution)/shard_map/ppermute | solution.py:93
  103.7 24.6 %collective-permute-start.4 = (f32[512,512]{1,0:T(8,128)S(1)}, f32[512,512]{1,0:T(8,128)S(1)}, u32[]{:S(2)}, u32[]{:S(2)}) collective-permute-start(f32[512,512]{1,0:T(8,128)S(1)} %add.110), channel_id=1, source_target_pairs={{0,128},{8,136},{16,144},{24,152},{32,160},{40,168},{48,176},{56,1... | collective-permute-start | bytes 3145736 | tf_op jit(solution)/shard_map/ppermute | solution.py:93
  105.8 26.8 %copy-start.7 = (s32[1,1,128]{2,1,0:T(1,128)S(1)}, s32[1,1,128]{2,1,0:T(1,128)}, u32[]{:S(2)}) copy-start(s32[1,1,128]{2,1,0:T(1,128)} %param.17) | copy-start | bytes 1540
  105.8 26.9 %copy-start.5 = (s32[1,1,1024]{2,1,0:T(1,128)S(1)}, s32[1,1,1024]{2,1,0:T(1,128)}, u32[]{:S(2)}) copy-start(s32[1,1,1024]{2,1,0:T(1,128)} %param.12) | copy-start | bytes 12292
  128.3 1.0 copy-start.2
  222.1 2.1 copy-start.3
  242.8 20.6 %copy-start.1 = (bf16[1024,512]{1,0:T(8,128)(2,1)S(1)}, bf16[1024,512]{1,0:T(8,128)(2,1)}, u32[]{:S(2)}) copy-start(bf16[1024,512]{1,0:T(8,128)(2,1)} %gather_fusion.2) | copy-start | bytes 3145732
  244.1 12.2 %collective-permute-start.5 = (bf16[1,256,512]{2,1,0:T(8,128)(2,1)S(1)}, bf16[1,256,512]{2,1,0:T(8,128)(2,1)S(1)}, u32[]{:S(2)}, u32[]{:S(2)}) collective-permute-start(bf16[1,256,512]{2,1,0:T(8,128)(2,1)S(1)} %get-tuple-element.10), channel_id=1, source_target_pairs={{0,8},{8,16},{16,24},{24,32},{32,40},{40,48},{48,56},{56,64},{64,7... | collective-permute-start | bytes 786440 | tf_op jit(solution)/shard_map/ppermute | solution.py:17
  246.1 10.2 %collective-permute-start.6 = (bf16[1,256,512]{2,1,0:T(8,128)(2,1)S(1)}, bf16[1,256,512]{2,1,0:T(8,128)(2,1)S(1)}, u32[]{:S(2)}, u32[]{:S(2)}) collective-permute-start(bf16[1,256,512]{2,1,0:T(8,128)(2,1)S(1)} %get-tuple-element.12), channel_id=1, source_target_pairs={{8,0},{16,8},{24,16},{32,24},{40,32},{48,40},{56,48},{64,56},{72,6... | collective-permute-start | bytes 786440 | tf_op jit(solution)/shard_map/ppermute | solution.py:19
  251.8 7.0 %collective-permute-start.7 = (bf16[1,256,512]{2,1,0:T(8,128)(2,1)S(1)}, bf16[1,256,512]{2,1,0:T(8,128)(2,1)S(1)}, u32[]{:S(2)}, u32[]{:S(2)}) collective-permute-start(bf16[1,256,512]{2,1,0:T(8,128)(2,1)S(1)} %get-tuple-element.11), channel_id=1, source_target_pairs={{0,1},{1,2},{2,3},{3,4},{4,5},{5,6},{6,7},{8,9},{9,10},{10,11},{11... | collective-permute-start | bytes 786440 | tf_op jit(solution)/shard_map/ppermute | solution.py:17
  255.0 8.3 %collective-permute-start.8 = (bf16[1,256,512]{2,1,0:T(8,128)(2,1)S(1)}, bf16[1,256,512]{2,1,0:T(8,128)(2,1)S(1)}, u32[]{:S(2)}, u32[]{:S(2)}) collective-permute-start(bf16[1,256,512]{2,1,0:T(8,128)(2,1)S(1)} %get-tuple-element.13), channel_id=1, source_target_pairs={{1,0},{2,1},{3,2},{4,3},{5,4},{6,5},{7,6},{9,8},{10,9},{11,10},{12... | collective-permute-start | bytes 786440 | tf_op jit(solution)/shard_map/ppermute | solution.py:19
Sparse Core Ops, SparseCore 0:
  132.8 77.9 all-reduce.1
